TPU v7x, 256 devices: a whole 4x4x8 slice. The times are simulated.
256 devices in a mesh: zero: 2 (over z_hi), expert: 128 (over y, x, z_lo, core).
Axes of the slice: x: 4, y: 4, z: 8 (z_hi: 2, z_lo: 4; z = z_hi * 4 + z_lo), core: 2. Of those that a mesh axis runs over, the one named last changes fastest.
Arguments:
- tokens: bfloat16 [32768, 2048], P(('zero', 'expert')), may hold values from -6 to 6
- cotangent: bfloat16 [32768, 2048], P(('zero', 'expert')), may hold values from -6 to 6
- expert_ids: int32 [32768, 2], P(('zero', 'expert')), may hold values from 0 to 127, all different within a row; in each aligned block of 128 rows (0 to 127, 128 to 255, ...) at most 4 rows name the same one
- gate_values: float32 [32768, 2], P(('zero', 'expert')), may hold values from 0.1 to 1
- w_gate: bfloat16 [128, 768, 2048], P('expert', 'zero'), may hold values from -0.125 to 0.125
- w_up: bfloat16 [128, 768, 2048], P('expert', 'zero'), may hold values from -0.125 to 0.125
- w_down: bfloat16 [128, 768, 2048], P('expert', 'zero'), may hold values from -0.21875 to 0.21875
Outputs:
- layer_out: bfloat16 [32768, 2048], P(('zero', 'expert'))
- token_grad: bfloat16 [32768, 2048], P(('zero', 'expert'))
- grad_gate: bfloat16 [128, 768, 2048], P('expert', 'zero')
- grad_up: bfloat16 [128, 768, 2048], P('expert', 'zero')
- grad_down: bfloat16 [128, 768, 2048], P('expert', 'zero')
Inputs may be any that keep to these rules, and one draw needn't show every extreme that they name: `expert_ids`: the 2 experts of a row differ. In each aligned block of 128 rows (the rows of one device) no expert is named more than 4 times, a bound that some block reaches.
All inputs are finite; a program needn't handle non-finite values.
Results may differ from a plain program's by a relative error of at most 0.0065.
Values may be sent and summed in bfloat16 or wider, within the bound.
A program may use at most 128 MiB of HBM per device.

v0:
```python
import jax
import jax.numpy as jnp
from jax import lax
from jax.sharding import PartitionSpec as P


def slot_positions(expert_ids, experts, capacity):
    assigned = expert_ids.reshape(-1)
    onehot = (assigned[:, None] == jnp.arange(experts, dtype=jnp.int32)[None, :]).astype(jnp.int32)
    earlier = jnp.cumsum(onehot, axis=0) - onehot
    ranking = jnp.sum(earlier * onehot, axis=1)
    return assigned * capacity + ranking


def swiglu_forward(row_data, weight_gate, weight_up):
    pre_gate = jnp.einsum("rd,fd->rf", row_data, weight_gate, preferred_element_type=jnp.float32)
    pre_up = jnp.einsum("rd,fd->rf", row_data, weight_up, preferred_element_type=jnp.float32)
    hidden = (jax.nn.silu(pre_gate) * pre_up).astype(jnp.bfloat16)
    return (pre_gate, pre_up, hidden)


def swiglu_backward(pre_gate, pre_up, cot_rows, weight_down):
    hidden_grad = jnp.einsum("rd,fd->rf", cot_rows, weight_down, preferred_element_type=jnp.float32)
    sigmoid = jax.nn.sigmoid(pre_gate)
    gate_grad = (hidden_grad * pre_up * (sigmoid * (1.0 + pre_gate * (1.0 - sigmoid)))).astype(
        jnp.bfloat16
    )
    up_grad = (hidden_grad * (pre_gate * sigmoid)).astype(jnp.bfloat16)
    return (gate_grad, up_grad)


def local(tokens, cotangent, expert_ids, gate_values, w_gate, w_up, w_down):
    experts = lax.axis_size("expert")
    tok_rows, model_width = tokens.shape
    top_k = expert_ids.shape[1]
    capacity = 2 * tok_rows * top_k // experts
    slot_count = experts * capacity
    position = slot_positions(expert_ids, experts, capacity)
    slot_match = position[:, None] == jnp.arange(slot_count, dtype=jnp.int32)[None, :]
    assignment_token = jnp.arange(tok_rows * top_k, dtype=jnp.int32) // top_k
    slot_owner = jnp.sum(jnp.where(slot_match, assignment_token[:, None], 0), axis=0)
    occupied = jnp.any(slot_match, axis=0)
    slot_gate = jnp.sum(jnp.where(slot_match, gate_values.reshape(-1)[:, None], 0.0), axis=0)
    send_rows = jnp.where(occupied[:, None], tokens[slot_owner], jnp.zeros((), tokens.dtype))
    send_rows = send_rows.reshape(experts, capacity, model_width)
    send_cot = (slot_gate[:, None] * cotangent[slot_owner].astype(jnp.float32)).astype(jnp.bfloat16)
    send_cot = send_cot.reshape(experts, capacity, model_width)
    got_rows, got_cot = (
        lax.all_to_all(send_rows, "expert", split_axis=0, concat_axis=0, tiled=True),
        lax.all_to_all(send_cot, "expert", split_axis=0, concat_axis=0, tiled=True),
    )
    expert_rows = got_rows.reshape(-1, model_width)
    cot_rows = got_cot.reshape(-1, model_width)
    full_gate, full_up, full_down = (
        lax.all_gather(w_gate, "zero", axis=1, tiled=True),
        lax.all_gather(w_up, "zero", axis=1, tiled=True),
        lax.all_gather(w_down, "zero", axis=1, tiled=True),
    )
    weight_gate, weight_up, weight_down = (full_gate[0], full_up[0], full_down[0])
    pre_gate, pre_up, hidden = swiglu_forward(expert_rows, weight_gate, weight_up)
    expert_out = jnp.einsum(
        "rf,fd->rd", hidden, weight_down, preferred_element_type=jnp.float32
    ).astype(jnp.bfloat16)
    gate_grad, up_grad = swiglu_backward(pre_gate, pre_up, cot_rows, weight_down)
    row_grad = (
        jnp.einsum("rf,fd->rd", gate_grad, weight_gate, preferred_element_type=jnp.float32)
        + jnp.einsum("rf,fd->rd", up_grad, weight_up, preferred_element_type=jnp.float32)
    ).astype(jnp.bfloat16)
    shares = lax.psum_scatter(
        jnp.stack(
            [
                jnp.einsum("rf,rd->fd", gate_grad, expert_rows, preferred_element_type=jnp.float32),
                jnp.einsum("rf,rd->fd", up_grad, expert_rows, preferred_element_type=jnp.float32),
                jnp.einsum("rf,rd->fd", hidden, cot_rows, preferred_element_type=jnp.float32),
            ],
            axis=1,
        ),
        "zero",
        scatter_dimension=0,
        tiled=True,
    )
    grad_gate = shares[:, 0, :].astype(jnp.bfloat16)[None]
    grad_up = shares[:, 1, :].astype(jnp.bfloat16)[None]
    grad_down = shares[:, 2, :].astype(jnp.bfloat16)[None]
    back_out, back_grad = (
        lax.all_to_all(
            expert_out.reshape(experts, capacity, model_width),
            "expert",
            split_axis=0,
            concat_axis=0,
            tiled=True,
        ),
        lax.all_to_all(
            row_grad.reshape(experts, capacity, model_width),
            "expert",
            split_axis=0,
            concat_axis=0,
            tiled=True,
        ),
    )
    picked_out = back_out.reshape(slot_count, model_width)[position].reshape(
        tok_rows, top_k, model_width
    )
    picked_grad = back_grad.reshape(slot_count, model_width)[position].reshape(
        tok_rows, top_k, model_width
    )
    layer_out = jnp.sum(gate_values[:, :, None] * picked_out.astype(jnp.float32), axis=1).astype(
        jnp.bfloat16
    )
    token_grad = jnp.sum(picked_grad.astype(jnp.float32), axis=1).astype(jnp.bfloat16)
    return (layer_out, token_grad, grad_gate, grad_up, grad_down)


def solution(mesh):
    return jax.shard_map(
        local,
        mesh=mesh,
        in_specs=(
            P(("zero", "expert"), None),
            P(("zero", "expert"), None),
            P(("zero", "expert"), None),
            P(("zero", "expert"), None),
            P("expert", "zero", None),
            P("expert", "zero", None),
            P("expert", "zero", None),
        ),
        out_specs=(
            P(("zero", "expert"), None),
            P(("zero", "expert"), None),
            P("expert", "zero", None),
            P("expert", "zero", None),
            P("expert", "zero", None),
        ),
        check_vma=False,
    )
```

profile of v0, /device:TPU:56, one launch (start us, length us, event | category | flops | bytes accessed | tf_op | source)
XLA Modules:
  0.0 900.8 jit_solution(4606816531052964824)
XLA Ops:
  10.1 2.5 gather_fusion
  14.8 3.9 broadcast_select_fusion
  18.7 13.2 %all-to-all-start = ((bf16[128,4,2048]{2,1,0:T(4,128)(2,1)}), bf16[128,4,2048]{2,1,0:T(4,128)(2,1)}, u32[]{:S(2)}, u32[]{:S(2)}) async-start(bf16[128,4,2048]{2,1,0:T(4,128)(2,1)} %broadcast_select_fusion), calls=%async_computation | async-start | bytes 4194304 | tf_op jit(solution)/shard_map/all_to_all | solution.py:49
  33.3 2.5 gather_fusion.2
  35.7 3.0 reshape.176
  38.8 4.3 multiply_convert_fusion
  43.1 99.4 %all-to-all-done = bf16[128,4,2048]{2,1,0:T(4,128)(2,1)} async-done(((bf16[128,4,2048]{2,1,0:T(4,128)(2,1)}), bf16[128,4,2048]{2,1,0:T(4,128)(2,1)}, u32[]{:S(2)}, u32[]{:S(2)}) %all-to-all-start) | async-done | bytes 2097184 | tf_op jit(solution)/shard_map/all_to_all | solution.py:49
  142.6 11.9 %all-to-all-start.2 = ((bf16[128,4,2048]{2,1,0:T(4,128)(2,1)}), bf16[128,4,2048]{2,1,0:T(4,128)(2,1)}, u32[]{:S(2)}, u32[]{:S(2)}) async-start(bf16[128,4,2048]{2,1,0:T(4,128)(2,1)} %multiply_convert_fusion), calls=%async_computation.2 | async-start | bytes 4194304 | tf_op jit(solution)/shard_map/all_to_all | solution.py:50
  155.7 2.5 reshape.168
  158.2 101.3 %all-to-all-done.2 = bf16[128,4,2048]{2,1,0:T(4,128)(2,1)} async-done(((bf16[128,4,2048]{2,1,0:T(4,128)(2,1)}), bf16[128,4,2048]{2,1,0:T(4,128)(2,1)}, u32[]{:S(2)}, u32[]{:S(2)}) %all-to-all-start.2) | async-done | bytes 2097184 | tf_op jit(solution)/shard_map/all_to_all | solution.py:50
  259.5 4.0 reshape.171
  263.5 4.9 fusion.6
  268.4 5.5 fusion
  273.9 56.8 %all-gather.4.cloned.1.call-done = bf16[1,768,2048]{2,1,0:T(8,128)(2,1)} async-done(((bf16[1,384,2048]{2,1,0:T(8,128)(2,1)}), bf16[1,768,2048]{2,1,0:T(8,128)(2,1)}) %all-gather.4.cloned.1.call-update) | async-done | bytes 3145744 | tf_op jit(solution)/shard_map/all_gather | solution.py:55
  330.7 5.4 multiply_convert_fusion.2
  341.6 7.0 pad_maximum_fusion
  348.6 3.9 fusion.12
  352.6 2.4 reshape.169
  354.9 10.5 %all-to-all-start.1 = ((bf16[128,4,2048]{2,1,0:T(4,128)(2,1)}), bf16[128,4,2048]{2,1,0:T(4,128)(2,1)S(1)}, u32[]{:S(2)}, u32[]{:S(2)}) async-start(bf16[128,4,2048]{2,1,0:T(4,128)(2,1)} %reshape.169), calls=%async_computation.1 | async-start | bytes 4194304 | tf_op jit(solution)/shard_map/all_to_all | solution.py:86
  365.4 4.1 fusion.4
  369.5 3.2 add_convert_fusion
  372.7 4.1 reshape.172
  376.8 433.9 %all-to-all-done.1 = bf16[128,4,2048]{2,1,0:T(4,128)(2,1)S(1)} async-done(((bf16[128,4,2048]{2,1,0:T(4,128)(2,1)}), bf16[128,4,2048]{2,1,0:T(4,128)(2,1)S(1)}, u32[]{:S(2)}, u32[]{:S(2)}) %all-to-all-start.1) | async-done | bytes 2097184 | tf_op jit(solution)/shard_map/all_to_all | solution.py:86
  812.0 12.3 %all-to-all-start.3 = ((bf16[128,4,2048]{2,1,0:T(4,128)(2,1)}), bf16[128,4,2048]{2,1,0:T(4,128)(2,1)}, u32[]{:S(2)}, u32[]{:S(2)}) async-start(bf16[128,4,2048]{2,1,0:T(4,128)(2,1)} %reshape.172), calls=%async_computation.3 | async-start | bytes 4194304 | tf_op jit(solution)/shard_map/all_to_all | solution.py:93
  824.5 2.5 reshape.170
  829.4 3.3 reshape.175
  832.8 38.5 %all-to-all-done.3 = bf16[128,4,2048]{2,1,0:T(4,128)(2,1)} async-done(((bf16[128,4,2048]{2,1,0:T(4,128)(2,1)}), bf16[128,4,2048]{2,1,0:T(4,128)(2,1)}, u32[]{:S(2)}, u32[]{:S(2)}) %all-to-all-start.3) | async-done | bytes 2097184 | tf_op jit(solution)/shard_map/all_to_all | solution.py:93
  871.3 2.5 reshape.173
  876.1 2.7 reshape.174
  878.8 4.6 reduce_sum.58
  883.4 3.9 multiply_reduce_fusion
  887.3 4.4 convert.8
  (67 shorter events, 21.6 us)
Async XLA Ops:
  7.2 2.9 copy-start
  7.2 256.3 %all-gather.6.cloned.1.call-start = ((), (), s32[]{:S(2)}) async-start(), calls=%async_computation.6 | async-start | bytes 4718592 | tf_op jit(solution)/shard_map/all_gather | solution.py:56
  18.7 14.0 %copy-start.9 = (f32[128,2]{0,1:T(2,128)S(1)}, f32[128,2]{0,1:T(2,128)}, u32[]{:S(2)}) copy-start(f32[128,2]{0,1:T(2,128)} %param.10) | copy-start | bytes 3076
  18.7 14.5 %copy-start.2 = (bf16[128,2048]{1,0:T(8,128)(2,1)S(1)}, bf16[128,2048]{1,0:T(8,128)(2,1)}, u32[]{:S(2)}) copy-start(bf16[128,2048]{1,0:T(8,128)(2,1)} %param.8) | copy-start | bytes 1572868
  18.7 123.8 %all-to-all-start = ((bf16[128,4,2048]{2,1,0:T(4,128)(2,1)}), bf16[128,4,2048]{2,1,0:T(4,128)(2,1)}, u32[]{:S(2)}, u32[]{:S(2)}) async-start(bf16[128,4,2048]{2,1,0:T(4,128)(2,1)} %broadcast_select_fusion), calls=%async_computation | async-start | bytes 4194304 | tf_op jit(solution)/shard_map/all_to_all | solution.py:49
  32.0 236.4 %all-gather.8.cloned.1.call-start = ((), (), s32[]{:S(2)}) async-start(), calls=%async_computation.7 | async-start | bytes 4718592 | tf_op jit(solution)/shard_map/all_gather | solution.py:57
  142.6 117.0 %all-to-all-start.2 = ((bf16[128,4,2048]{2,1,0:T(4,128)(2,1)}), bf16[128,4,2048]{2,1,0:T(4,128)(2,1)}, u32[]{:S(2)}, u32[]{:S(2)}) async-start(bf16[128,4,2048]{2,1,0:T(4,128)(2,1)} %multiply_convert_fusion), calls=%async_computation.2 | async-start | bytes 4194304 | tf_op jit(solution)/shard_map/all_to_all | solution.py:50
  154.5 176.2 %all-gather.4.cloned.1.call-start = ((), (), s32[]{:S(2)}) async-start(), calls=%async_computation.5 | async-start | bytes 4718592 | tf_op jit(solution)/shard_map/all_gather | solution.py:55
  155.2 732.1 %reduce-scatter.2.cloned.1.call-start = ((), (), s32[]{:S(2)}) async-start(), calls=%async_computation.8 | async-start | bytes 28311552 | tf_op jit(solution)/shard_map/reduce_scatter | solution.py:69
  330.6 5.4 copy-start.5
  336.0 1.9 copy-start.7
  336.0 3.7 copy-start.6
  354.9 455.7 %all-to-all-start.1 = ((bf16[128,4,2048]{2,1,0:T(4,128)(2,1)}), bf16[128,4,2048]{2,1,0:T(4,128)(2,1)S(1)}, u32[]{:S(2)}, u32[]{:S(2)}) async-start(bf16[128,4,2048]{2,1,0:T(4,128)(2,1)} %reshape.169), calls=%async_computation.1 | async-start | bytes 4194304 | tf_op jit(solution)/shard_map/all_to_all | solution.py:86
  365.4 4.1 copy-start.10
  376.8 447.4 %copy-start.8 = (s32[128,2]{0,1:T(2,128)S(1)}, s32[128,2]{0,1:T(2,128)}, u32[]{:S(2)}) copy-start(s32[128,2]{0,1:T(2,128)} %param.9) | copy-start | bytes 3076
  810.7 1.3 copy-start.3
  812.0 59.3 %all-to-all-start.3 = ((bf16[128,4,2048]{2,1,0:T(4,128)(2,1)}), bf16[128,4,2048]{2,1,0:T(4,128)(2,1)}, u32[]{:S(2)}, u32[]{:S(2)}) async-start(bf16[128,4,2048]{2,1,0:T(4,128)(2,1)} %reshape.172), calls=%async_computation.3 | async-start | bytes 4194304 | tf_op jit(solution)/shard_map/all_to_all | solution.py:93
  876.1 7.2 copy-start.4
  891.8 2.3 copy-start.1
Sparse Core Ops, SparseCore 0:
  9.8 106.6 all-gather.5
  118.3 117.4 all-gather.7
  237.7 92.9 all-gather.3
  348.7 269.8 reduce-scatter.1
where the time goes:
time: 914 us; the launch traced here: 901 us
  waiting for transfers between devices  732 us (80%)
  starting transfers between devices  48.5 us (5%)
  local copies, waits for them, and re-layouts  44.5 us (5%)
  matrix products  32.4 us (4%)
  other arithmetic  29.2 us (3%)
  between operations  14.3 us (2%)
    all_to_all x1, waiting for transfers between devices, local(): lax.all_to_all(expert_out.reshape(experts, capacity, model_width), 'exper...  434 us
    all_to_all x1, waiting for transfers between devices, local(): lax.all_to_all(send_cot, 'expert', split_axis=0, concat_axis=0, tiled=True)  101 us
    all_to_all x1, waiting for transfers between devices, local(): lax.all_to_all(send_rows, 'expert', split_axis=0, concat_axis=0, tiled=True)  99.4 us
    all_gather x1, waiting for transfers between devices, local(): lax.all_gather(w_gate, 'zero', axis=1, tiled=True)  56.8 us
    all_to_all x1, waiting for transfers between devices, local(): lax.all_to_all(row_grad.reshape(experts, capacity, model_width), 'expert'...  38.5 us
  transfers between devices with their start and end apart: 8, of which 5 were waited for; matrix products, arithmetic and copies ran while one was open for 9% of the time, Pallas kernels for 0%

commit v1 on v0

v1 whole, which is shorter than its diff:
```python
import functools

import jax
import jax.numpy as jnp
from jax import lax
from jax.experimental import pallas as pl
from jax.experimental.pallas import tpu as pltpu
from jax.sharding import PartitionSpec as P

MESH = pl.DeviceIdType.MESH
BF16, F32, I32 = jnp.bfloat16, jnp.float32, jnp.int32

RING = 8
PLANE = 32
WIDE = 256
CAP = 4
SOURCE_ROWS = RING * CAP
FROM_LEFT = {0: 0, 1: 1, 2: 3, 3: 5, 4: 7}
FROM_RIGHT = {0: 0, 1: 2, 2: 4, 3: 6, 4: 7}


def dot(a, b):
    return lax.dot_general(a, b, (((1,), (0,)), ((), ())), preferred_element_type=F32)


def dot_nt(a, b):
    return lax.dot_general(a, b, (((1,), (1,)), ((), ())), preferred_element_type=F32)


def kernel(
    ids_c, ids_r, gate_r, tok, cot, wg, wu, wd,
    layer_out, token_grad, grad_gate, grad_up, grad_down,
    G, S, X, Q, RS, WB, F, H, T, D, C, GR, M,
    load_sem, wload_sem, meta_send, meta_recv, ring_send, ring_recv,
    out_send, out_recv, back_send, back_recv, rs_send, rs_recv, store_sem, wstore_sem,
):
    n = G.shape[0]
    tok_rows = G.shape[3]
    expert = lax.axis_index("expert")
    core = expert % 2
    z_lo = (expert // 2) % 4
    x = (expert // 8) % 4
    y = expert // 32
    z = lax.axis_index("zero") * 4 + z_lo

    def along_z(step):
        to = (z + step + RING) % RING
        return (to // 4, ((y * 4 + x) * 4 + to % 4) * 2 + core)

    def in_plane(j, sign):
        to_y = (y + sign * (j // 8) + 4) % 4
        to_x = (x + sign * ((j // 2) % 4) + 4) % 4
        to_c = (core + j % 2) % 2
        return (z // 4, ((to_y * 4 + to_x) * 4 + z_lo) * 2 + to_c)

    def columns(c):
        return pl.ds(pl.multiple_of(c * WIDE, WIDE), WIDE)

    def loads(c):
        return [
            pltpu.make_async_copy(ref.at[:, columns(c)], G.at[c, 0, a], load_sem.at[c, a])
            for a, ref in enumerate((tok, cot))
        ]

    def start_load(c, carry):
        for copy in loads(c):
            copy.start()
        return carry

    lax.fori_loop(0, n, start_load, 0)

    barrier = pltpu.get_barrier_semaphore()

    def greet(j, carry):
        pl.semaphore_signal(barrier, inc=1, device_id=in_plane(j, 1), device_id_type=MESH)
        return carry

    lax.fori_loop(1, PLANE, greet, 0)
    for step in range(1, RING):
        pl.semaphore_signal(barrier, inc=1, device_id=along_z(step), device_id_type=MESH)

    def start_weights(c, carry):
        for i, ref in enumerate((wg, wu, wd)):
            pltpu.make_async_copy(ref.at[0, :, columns(c)], WB.at[i, c], wload_sem).start()
        return carry

    lax.fori_loop(0, n, start_weights, 0)

    earlier = lax.broadcasted_iota(I32, (tok_rows, tok_rows), 0) < lax.broadcasted_iota(
        I32, (tok_rows, tok_rows), 1
    )
    for k in range(2):
        same = jnp.zeros((tok_rows, tok_rows), F32)
        for k2 in range(2):
            same += jnp.where((ids_c[:, k2 : k2 + 1] == ids_r[k : k + 1, :]) & earlier, 1.0, 0.0)
        slot = jnp.sum(same, axis=0, keepdims=True)
        M[0, k : k + 1, :] = ids_r[k : k + 1, :].astype(F32) * CAP + slot
    M[0, 2:4, :] = gate_r[...]
    M[0, 4:8, :] = jnp.zeros((4, tok_rows), F32)

    pl.semaphore_wait(barrier, PLANE - 1 + RING - 1)

    def remote(src, dst, send, recv, to):
        return pltpu.make_async_remote_copy(
            src_ref=src, dst_ref=dst, send_sem=send, recv_sem=recv, device_id=to, device_id_type=MESH
        )

    right, left = along_z(1), along_z(-1)

    def ring_copies(c, hop):
        got_l, got_r = FROM_LEFT[hop - 1], FROM_RIGHT[hop - 1]
        to_l, to_r = FROM_LEFT[hop], FROM_RIGHT[hop]
        if hop < 4:
            return (
                remote(G.at[c, got_l], G.at[c, to_l], ring_send.at[c, 2 * hop - 2], ring_recv.at[c, to_l], right),
                remote(G.at[c, got_r], G.at[c, to_r], ring_send.at[c, 2 * hop - 1], ring_recv.at[c, to_r], left),
            )
        return (
            remote(G.at[c, got_l, 0], G.at[c, 7, 0], ring_send.at[c, 6], ring_recv.at[c, 7], right),
            remote(G.at[c, got_r, 1], G.at[c, 7, 1], ring_send.at[c, 7], ring_recv.at[c, 0], left),
        )

    def ring_hop(c, hop):
        if hop == 1:
            for copy in loads(c):
                copy.wait()
            for copy in ring_copies(c, 1):
                copy.start()
        else:
            for before, copy in zip(ring_copies(c, hop - 1), ring_copies(c, hop)):
                before.wait_recv()
                copy.start()

    def ring_end(c):
        for copy in ring_copies(c, 4):
            copy.wait_recv()

    ring_hop(0, 1)
    metas = []
    for slot, step in enumerate((0, 1, -1, 2, -2, 3, -3, 4)):
        if step:
            metas.append(remote(M.at[0], M.at[slot], meta_send.at[slot], meta_recv.at[slot], along_z(step)))
    for copy in metas:
        copy.start()
    ring_hop(1, 1)
    ring_hop(0, 2)
    F[...] = jnp.zeros(F.shape, F32)
    for copy in metas:
        copy.wait_recv()
    ring_hop(0, 3)

    def place(position, i):
        e = position.astype(I32) // CAP
        s = position.astype(I32) % CAP
        mine = ((e // 2) % 4) == z_lo
        j = ((e // 32 - y + 4) % 4) * 8 + ((e // 8 - x + 4) % 4) * 2 + (e - core + 2) % 2
        return jnp.where(mine, j * 16 + i * CAP + s, -1)

    half = PLANE * 16
    row_id = lax.broadcasted_iota(I32, (half, tok_rows), 0)
    col_id = lax.broadcasted_iota(I32, (tok_rows, half), 1)
    for g in range(2):
        gates = jnp.zeros((half, tok_rows), F32)
        for i in range(4):
            m = M[4 * g + i]
            mt = jnp.transpose(m)
            tokens_i = slice(i * tok_rows, (i + 1) * tok_rows)
            first, second = row_id == place(m[0:1], i), row_id == place(m[1:2], i)
            D[g, :, tokens_i] = jnp.where(first | second, 1.0, 0.0).astype(BF16)
            gates += jnp.where(first, m[2:3], 0.0) + jnp.where(second, m[3:4], 0.0)
            first, second = col_id == place(mt[:, 0:1], i), col_id == place(mt[:, 1:2], i)
            C[0, g, tokens_i, :] = jnp.where(first | second, 1.0, 0.0).astype(BF16)
            weight = jnp.where(first, mt[:, 2:3], 0.0) + jnp.where(second, mt[:, 3:4], 0.0)
            high = weight.astype(BF16)
            C[1, g, tokens_i, :] = high
            C[2, g, tokens_i, :] = (weight - high.astype(F32)).astype(BF16)
        GR[g] = jnp.broadcast_to(jnp.sum(gates, axis=1, keepdims=True), (half, 128))
    ring_hop(0, 4)

    def pick(c):
        for g in range(2):
            rows = slice(16 * g, 16 * g + 16)
            for a in range(2):
                block = G[c, 4 * g : 4 * g + 4, a].reshape(4 * tok_rows, WIDE)
                picked = dot(D[g], block)
                if a == 1:
                    picked = picked * jnp.concatenate([GR[g]] * (WIDE // 128), axis=1)
                S[c, :, a, rows, :] = picked.astype(BF16).reshape(PLANE, 16, WIDE)
        X[c, 0] = S[c, 0]

    def send(c, dst, sign, send_sem, recv_sem):
        def one(j, carry):
            remote(S.at[c, j], dst.at[c, j], send_sem.at[c], recv_sem.at[c], in_plane(j, sign)).start()
            return carry

        lax.fori_loop(1, PLANE, one, 0)

    def all_of(c, dst, send_sem, recv_sem):
        others = pl.ds(1, PLANE - 1)
        return remote(S.at[c, others], dst.at[c, others], send_sem.at[c], recv_sem.at[c], right)

    def row_tile(c, a, m):
        return X[c, pl.ds(8 * m, 8), a].reshape(8 * SOURCE_ROWS, WIDE)

    def tile_rows(m):
        return pl.ds(pl.multiple_of(m * 256, 256), 256)

    def unit_cols(i):
        units = WB.shape[2]
        return slice(i * units, (i + 1) * units)

    def before_act(c):
        all_of(c, X, out_send, out_recv).wait_recv()

        def tile(m, carry):
            rows, cots = row_tile(c, 0, m), row_tile(c, 1, m)
            for i, block in enumerate((rows, rows, cots)):
                F[tile_rows(m), unit_cols(i)] += dot_nt(block, WB[i, c])
            return carry

        lax.fori_loop(0, 4, tile, 0)

    pltpu.make_async_copy(WB, WB, wload_sem).wait()

    def way_out(t, carry):
        @pl.when(t + 2 < n)
        def _():
            ring_hop(t + 2, 1)

        @pl.when(t + 1 < n)
        def _():
            ring_hop(t + 1, 2)

        ring_end(t)
        pick(t)
        send(t, X, 1, out_send, out_recv)

        @pl.when(t + 1 < n)
        def _():
            ring_hop(t + 1, 3)

        @pl.when(t >= 2)
        def _():
            before_act(t - 2)

        @pl.when(t + 1 < n)
        def _():
            ring_hop(t + 1, 4)

        return carry

    lax.fori_loop(0, n, way_out, 0)
    before_act(n - 2)
    before_act(n - 1)

    def activate(m, carry):
        pre_gate, pre_up, hidden_grad = (F[tile_rows(m), unit_cols(i)] for i in range(3))
        sigmoid = jax.nn.sigmoid(pre_gate)
        silu = pre_gate * sigmoid
        hidden = silu * pre_up
        gate_grad = hidden_grad * pre_up * (sigmoid * (1.0 + pre_gate * (1.0 - sigmoid)))
        up_grad = hidden_grad * silu
        for i, v in enumerate((gate_grad, up_grad, hidden)):
            H[i, m] = v.astype(BF16)
            T[i, m] = jnp.transpose(v).astype(BF16)
        return carry

    lax.fori_loop(0, 4, activate, 0)

    def answer(c, carry):
        all_of(c, X, out_send, out_recv).wait_send()

        def tile(m, carry):
            expert_out = dot(H[2, m], WB[2, c])
            row_grad = dot(H[0, m], WB[0, c]) + dot(H[1, m], WB[1, c])
            S[c, pl.ds(8 * m, 8), 0] = expert_out.astype(BF16).reshape(8, SOURCE_ROWS, WIDE)
            S[c, pl.ds(8 * m, 8), 1] = row_grad.astype(BF16).reshape(8, SOURCE_ROWS, WIDE)
            return carry

        lax.fori_loop(0, 4, tile, 0)
        Q[c, 0] = S[c, 0]
        send(c, Q, -1, back_send, back_recv)
        return carry

    lax.fori_loop(0, n, answer, 0)

    def ring_sent(c, carry):
        for hop in range(1, 5):
            for copy in ring_copies(c, hop):
                copy.wait_send()
        return carry

    lax.fori_loop(0, n, ring_sent, 0)

    def part_cols(c, a):
        return columns((c % 2) * 2 + a)

    def combine(c):
        all_of(c, Q, back_send, back_recv).wait_recv()
        for g in range(2):
            rows = slice(16 * g, 16 * g + 16)
            frames = slice(4 * tok_rows * g, 4 * tok_rows * (g + 1))
            outs = Q[c, :, 0, rows, :].reshape(half, WIDE)
            F[frames, part_cols(c, 0)] = dot(C[1, g], outs) + dot(C[2, g], outs)
            grads = Q[c, :, 1, rows, :].reshape(half, WIDE)
            F[frames, part_cols(c, 1)] = dot(C[0, g], grads)

    def part(c, slot, a):
        return F[slot * tok_rows : (slot + 1) * tok_rows, part_cols(c, a)]

    def rs_copies(c, hop):
        if hop == 1:
            return (
                remote(G.at[c, 7, 0], RS.at[c, 0, 3, 0], rs_send.at[c, 0, 3], rs_recv.at[c, 0, 3], right),
                remote(G.at[c, 7, 1], RS.at[c, 1, 3, 1], rs_send.at[c, 1, 3], rs_recv.at[c, 1, 3], left),
            )
        at, to = 5 - hop, 4 - hop
        return tuple(
            remote(RS.at[c, way, at], RS.at[c, way, to], rs_send.at[c, way, to], rs_recv.at[c, way, to], whom)
            for way, whom in enumerate((right, left))
        )

    def rs_hop(c, hop):
        copies = rs_copies(c, hop)
        if hop == 1:
            for a in range(2):
                G[c, 7, a] = part(c, 7, a).astype(BF16)
                copies[a].start()
            return
        at = 5 - hop
        for way, slots in enumerate((FROM_RIGHT, FROM_LEFT)):
            rs_copies(c, hop - 1)[way].wait_recv()
            for a in range(2):
                total = part(c, slots[at], a)
                if hop > 2 or a == way:
                    total = total + RS[c, way, at, a].astype(F32)
                RS[c, way, at, a] = total.astype(BF16)
            copies[way].start()

    def stores(c):
        return [
            pltpu.make_async_copy(G.at[c, 0, a], ref.at[:, columns(c)], store_sem.at[c, a])
            for a, ref in enumerate((layer_out, token_grad))
        ]

    def rs_end(c):
        for copy in rs_copies(c, 4):
            copy.wait_recv()
        for a, copy in enumerate(stores(c)):
            total = part(c, 0, a) + RS[c, 0, 0, a].astype(F32) + RS[c, 1, 0, a].astype(F32)
            G[c, 0, a] = total.astype(BF16)
            copy.start()

    def wstore(c, i):
        ref = (grad_gate, grad_up, grad_down)[i]
        return pltpu.make_async_copy(WB.at[i, c], ref.at[0, :, columns(c)], wstore_sem.at[c, i])

    def weight_grad(c, i):
        a = 1 if i == 2 else 0
        total = dot(T[i, 0], row_tile(c, a, 0))
        for m in range(1, 4):
            total += dot(T[i, m], row_tile(c, a, m))
        WB[i, c] = total.astype(BF16)
        wstore(c, i).start()

    def way_back(c, carry):
        combine(c)
        rs_hop(c, 1)

        @pl.when(c >= 1)
        def _():
            rs_hop(c - 1, 3)

        weight_grad(c, 0)
        rs_hop(c, 2)
        weight_grad(c, 1)

        @pl.when(c >= 1)
        def _():
            rs_hop(c - 1, 4)

        weight_grad(c, 2)

        @pl.when(c >= 1)
        def _():
            rs_end(c - 1)

        return carry

    lax.fori_loop(0, n, way_back, 0)
    rs_hop(n - 1, 3)
    rs_hop(n - 1, 4)
    rs_end(n - 1)

    def finish(c, carry):
        for copy in stores(c):
            copy.wait()
        for i in range(3):
            wstore(c, i).wait()
        all_of(c, Q, back_send, back_recv).wait_send()
        for hop in range(1, 5):
            for copy in rs_copies(c, hop):
                copy.wait_send()
        return carry

    lax.fori_loop(0, n, finish, 0)
    for copy in metas:
        copy.wait_send()


def local(tokens, cotangent, expert_ids, gate_values, w_gate, w_up, w_down):
    tok_rows, width = tokens.shape
    hidden = w_gate.shape[1]
    n = width // WIDE
    rows = PLANE * SOURCE_ROWS
    half = PLANE * 16
    sem = pltpu.SemaphoreType.DMA
    vmem, hbm = pl.BlockSpec(memory_space=pltpu.VMEM), pl.BlockSpec(memory_space=pl.ANY)
    return pl.pallas_call(
        kernel,
        out_shape=[jax.ShapeDtypeStruct(v.shape, BF16) for v in (tokens, cotangent, w_gate, w_up, w_down)],
        in_specs=[vmem] * 3 + [hbm] * 5,
        out_specs=[hbm] * 5,
        scratch_shapes=[
            pltpu.VMEM((n, RING, 2, tok_rows, WIDE), BF16),
            pltpu.VMEM((n, PLANE, 2, SOURCE_ROWS, WIDE), BF16),
            pltpu.VMEM((n, PLANE, 2, SOURCE_ROWS, WIDE), BF16),
            pltpu.VMEM((n, PLANE, 2, SOURCE_ROWS, WIDE), BF16),
            pltpu.VMEM((n, 2, 4, 2, tok_rows, WIDE), BF16),
            pltpu.VMEM((3, n, hidden, WIDE), BF16),
            pltpu.VMEM((rows, max(3 * hidden, 4 * WIDE)), F32),
            pltpu.VMEM((3, 4, rows // 4, hidden), BF16),
            pltpu.VMEM((3, 4, hidden, rows // 4), BF16),
            pltpu.VMEM((2, half, 4 * tok_rows), BF16),
            pltpu.VMEM((3, 2, 4 * tok_rows, half), BF16),
            pltpu.VMEM((2, half, 128), F32),
            pltpu.VMEM((RING, 8, tok_rows), F32),
            sem((n, 2)), sem, sem((RING,)), sem((RING,)), sem((n, 8)), sem((n, 8)),
            sem((n,)), sem((n,)), sem((n,)), sem((n,)), sem((n, 2, 4)), sem((n, 2, 4)), sem((n, 2)), sem((n, 3)),
        ],
        compiler_params=pltpu.CompilerParams(
            collective_id=0, has_side_effects=True, vmem_limit_bytes=63 * 2**20
        ),
    )(expert_ids, expert_ids.T, gate_values.T, tokens, cotangent, w_gate, w_up, w_down)


def solution(mesh):
    rows = P(("zero", "expert"), None)
    weights = P("expert", "zero", None)
    return jax.shard_map(
        local,
        mesh=mesh,
        in_specs=(rows, rows, rows, rows, weights, weights, weights),
        out_specs=(rows, rows, weights, weights, weights),
        check_vma=False,
    )
```

time: 914 us -> 297 us (0.32); the launches traced: 901 us -> 296 us
  waiting for transfers between devices: 732 us -> 0 us
  Pallas kernels: 0 us -> 285 us
  starting transfers between devices: 48.5 us -> 0 us
  local copies, waits for them, and re-layouts: 44.5 us -> 10.4 us
  matrix products: 32.4 us -> 0 us
  other arithmetic: 29.2 us -> 0 us
  between operations: 14.3 us -> 0.65 us
    all_to_all x4 -> x0, waiting for transfers between devices: 673 us -> none  [the longest x1 434 us: local(): lax.all_to_all(expert_out.reshape(experts, capacity, model_width), 'exper...]
    pallas_call x0 -> x1, Pallas kernels: none -> 285 us  [local(): pl.pallas_call(kernel, out_shape=[jax.ShapeDtypeStruct(v.shape, BF16) for...]
    all_gather x3 -> x0, waiting for transfers between devices: 56.8 us -> none  [the longest x1 56.8 us: local(): lax.all_gather(w_gate, 'zero', axis=1, tiled=True)]
    all_to_all x4 -> x0, starting transfers between devices: 47.9 us -> none  [the longest x1 13.2 us: local(): lax.all_to_all(send_rows, 'expert', split_axis=0, concat_axis=0, tiled=True)]
    dot_general x9 -> x0, matrix products: 32.4 us -> none  [the longest x1 5.49 us: swiglu_backward(): jnp.einsum('rd,fd->rf', cot_rows, weight_down, preferred_element_type=jnp...]
    reshape x8 -> x0, local copies, waits for them, and re-layouts: 20.9 us -> none  [the longest x2 5.21 us: local(): back_grad.reshape(slot_count, model_width)[position]]
    gather x5 -> x0, local copies, waits for them, and re-layouts: 11.8 us -> none  [the longest x2 4.7 us: local(): tokens[slot_owner]]
    another operation x5 -> x0, other arithmetic: 11.7 us -> none  [the longest x1 6.98 us: local(): jnp.stack([jnp.einsum('rf,rd->fd', gate_grad, expert_rows, preferred_elem...]
  transfers between devices with their start and end apart: 8 -> 0, of which waited for: 5 -> 0; matrix products, arithmetic and copies ran while one was open for 9% -> 0% of each run, Pallas kernels for 0% -> 0%
where the time goes in v1:
time: 297 us; the launch traced here: 296 us
  Pallas kernels  285 us (96%)
  local copies, waits for them, and re-layouts  10.4 us (4%)
    pallas_call x1, Pallas kernels, local(): pl.pallas_call(kernel, out_shape=[jax.ShapeDtypeStruct(v.shape, BF16) for...  285 us
    unnamed x12, local copies, waits for them, and re-layouts  10.4 us

profile of v1, /device:TPU:56, one launch (start us, length us, event | category | flops | bytes accessed | tf_op | source)
XLA Modules:
  0.0 296.3 jit_solution(9378492579854614886)
XLA Ops:
  0.6 1.4 copy.12.ids_c
  2.0 285.3 %shard_map.110 = (bf16[128,2048]{1,0:T(8,128)(2,1)}, bf16[128,2048]{1,0:T(8,128)(2,1)}, bf16[1,384,2048]{2,1,0:T(8,128)(2,1)}, bf16[1,384,2048]{2,1,0:T(8,128)(2,1)}, bf16[1,384,2048]{2,1,0:T(8,128)(2,1)}) custom-call(s32[128,2]{1,0:T(8,128)} %copy.12.ids_c, s32[2,128]{1,0:T(2,128)} %bitcast.2, f32[2,128]{1,0:T(2,128)} %bitcast.3, bf16[128,2048]{1,0:T(8,128)(2,1)} %tok.1, ...), custom_call_target="tpu_custom_call" | custom-call | tf_op jit(solution)/shard_map/pallas_call | solution.py:419
  287.4 0.0 copy-start.2
  287.4 2.0 copy.18
  289.4 1.9 copy.19
  291.2 0.0 copy-done.2
  291.2 0.0 copy-start.1
  291.2 1.1 copy.20
  292.4 0.8 copy-done.1
  293.2 0.0 copy-start
  293.2 1.1 copy.21
  294.4 0.8 copy-done
  295.2 1.1 copy.22
Async XLA Ops:
  287.4 3.9 %copy-start.2 = (bf16[1,384,2048]{2,1,0:T(8,128)(2,1)S(1)}, bf16[1,384,2048]{2,1,0:T(8,128)(2,1)}, u32[]{:S(2)}) copy-start(bf16[1,384,2048]{2,1,0:T(8,128)(2,1)} %get-tuple-element.12) | copy-start | bytes 4718596
  291.2 2.0 copy-start.1
  293.2 2.0 copy-start

commit v2 on v1

v2 whole, which is shorter than its diff:
```python
import functools

import jax
import jax.numpy as jnp
from jax import lax
from jax.experimental import pallas as pl
from jax.experimental.pallas import tpu as pltpu
from jax.sharding import PartitionSpec as P

MESH = pl.DeviceIdType.MESH
BF16, F32, I32 = jnp.bfloat16, jnp.float32, jnp.int32

RING = 8
PLANE = 32
WIDE = 256
CAP = 4
SOURCE_ROWS = RING * CAP
FROM_LEFT = {0: 0, 1: 1, 2: 3, 3: 5, 4: 7}
FROM_RIGHT = {0: 0, 1: 2, 2: 4, 3: 6, 4: 7}


def dot(a, b):
    return lax.dot_general(a, b, (((1,), (0,)), ((), ())), preferred_element_type=F32)


def dot_nt(a, b):
    return lax.dot_general(a, b, (((1,), (1,)), ((), ())), preferred_element_type=F32)


def kernel(
    ids_r, gate_r, tok, cot, wg, wu, wd,
    layer_out, token_grad, grad_gate, grad_up, grad_down,
    G, S, X, Q, RS, WB, F, H, T, D, C, GR, M,
    load_sem, wload_sem, meta_send, meta_recv, ring_send, ring_recv,
    out_send, out_recv, back_send, back_recv, rs_send, rs_recv, store_sem, wstore_sem,
):
    n = G.shape[0]
    tok_rows = G.shape[3]
    expert = lax.axis_index("expert")
    core = expert % 2
    z_lo = (expert // 2) % 4
    x = (expert // 8) % 4
    y = expert // 32
    z = lax.axis_index("zero") * 4 + z_lo

    def along_z(step):
        to = (z + step + RING) % RING
        return (to // 4, ((y * 4 + x) * 4 + to % 4) * 2 + core)

    def in_plane(j, sign):
        to_y = (y + sign * (j // 8) + 4) % 4
        to_x = (x + sign * ((j // 2) % 4) + 4) % 4
        to_c = (core + j % 2) % 2
        return (z // 4, ((to_y * 4 + to_x) * 4 + z_lo) * 2 + to_c)

    def columns(c):
        return pl.ds(pl.multiple_of(c * WIDE, WIDE), WIDE)

    def loads(c):
        return [
            pltpu.make_async_copy(ref.at[:, columns(c)], G.at[c, 0, a], load_sem.at[c, a])
            for a, ref in enumerate((tok, cot))
        ]

    def start_load(c, carry):
        for copy in loads(c):
            copy.start()
        return carry

    lax.fori_loop(0, n, start_load, 0)

    barrier = pltpu.get_barrier_semaphore()

    def greet(j, carry):
        pl.semaphore_signal(barrier, inc=1, device_id=in_plane(j, 1), device_id_type=MESH)
        return carry

    lax.fori_loop(1, PLANE, greet, 0)
    for step in range(1, RING):
        pl.semaphore_signal(barrier, inc=1, device_id=along_z(step), device_id_type=MESH)

    def start_weights(c, carry):
        for i, ref in enumerate((wg, wu, wd)):
            pltpu.make_async_copy(ref.at[0, :, columns(c)], WB.at[i, c], wload_sem).start()
        return carry

    lax.fori_loop(0, n, start_weights, 0)

    earlier = lax.broadcasted_iota(I32, (tok_rows, tok_rows), 0) < lax.broadcasted_iota(
        I32, (tok_rows, tok_rows), 1
    )
    M[0] = jnp.zeros((8, tok_rows), F32)
    M[0, 0:2, :] = ids_r[...].astype(F32)
    ids_c = jnp.transpose(M[0])
    for k in range(2):
        own = ids_r[k : k + 1, :].astype(F32)
        same = jnp.zeros((tok_rows, tok_rows), F32)
        for k2 in range(2):
            same += jnp.where((ids_c[:, k2 : k2 + 1] == own) & earlier, 1.0, 0.0)
        slot = jnp.sum(same, axis=0, keepdims=True)
        M[0, k : k + 1, :] = own * CAP + slot
    M[0, 2:4, :] = gate_r[...]

    pl.semaphore_wait(barrier, PLANE - 1 + RING - 1)

    def remote(src, dst, send, recv, to):
        return pltpu.make_async_remote_copy(
            src_ref=src, dst_ref=dst, send_sem=send, recv_sem=recv, device_id=to, device_id_type=MESH
        )

    right, left = along_z(1), along_z(-1)

    def ring_copies(c, hop, a):
        got_l, got_r = FROM_LEFT[hop - 1], FROM_RIGHT[hop - 1]
        to_l, to_r = FROM_LEFT[hop], FROM_RIGHT[hop]
        ways = (
            (got_l, to_l, 2 * hop - 2, right),
            (got_r, to_r, 2 * hop - 1, left),
        )
        if hop == 4:
            ways = ways[a : a + 1]
        return [
            remote(G.at[c, got, a], G.at[c, to, a], ring_send.at[c, number, a], ring_recv.at[c, to, a], whom)
            for got, to, number, whom in ways
        ]

    def ring_hop(c, hop):
        for a in range(2):
            if hop == 1:
                loads(c)[a].wait()
            else:
                for copy in came_in(c, hop - 1, a, hop == 4):
                    copy.wait_recv()
            for copy in ring_copies(c, hop, a):
                copy.start()

    def came_in(c, hop, a, forwarded=False):
        copies = ring_copies(c, hop, a)
        return copies[a : a + 1] if forwarded else copies

    def ring_end(c):
        for a in range(2):
            ring_copies(c, 3, a)[1 - a].wait_recv()
        for a in range(2):
            ring_copies(c, 4, a)[0].wait_recv()

    ring_hop(0, 1)
    metas = []
    for slot, step in enumerate((0, 1, -1, 2, -2, 3, -3, 4)):
        if step:
            metas.append(remote(M.at[0], M.at[slot], meta_send.at[slot], meta_recv.at[slot], along_z(step)))
    for copy in metas:
        copy.start()
    ring_hop(0, 2)
    for copy in metas:
        copy.wait_recv()

    def place(position, i):
        e = position.astype(I32) // CAP
        s = position.astype(I32) % CAP
        mine = ((e // 2) % 4) == z_lo
        j = ((e // 32 - y + 4) % 4) * 8 + ((e // 8 - x + 4) % 4) * 2 + (e - core + 2) % 2
        return jnp.where(mine, j * 16 + i * CAP + s, -1)

    half = PLANE * 16

    def build_pick(g):
        row_id = lax.broadcasted_iota(I32, (half, tok_rows), 0)
        gates = jnp.zeros((half, tok_rows), F32)
        for i in range(4):
            m = M[4 * g + i]
            first, second = row_id == place(m[0:1], i), row_id == place(m[1:2], i)
            D[g, :, i * tok_rows : (i + 1) * tok_rows] = jnp.where(first | second, 1.0, 0.0).astype(BF16)
            gates += jnp.where(first, m[2:3], 0.0) + jnp.where(second, m[3:4], 0.0)
        GR[g] = jnp.broadcast_to(jnp.sum(gates, axis=1, keepdims=True), (half, 128))

    def build_put(g):
        col_id = lax.broadcasted_iota(I32, (tok_rows, half), 1)
        for i in range(4):
            mt = jnp.transpose(M[4 * g + i])
            tokens_i = slice(i * tok_rows, (i + 1) * tok_rows)
            first, second = col_id == place(mt[:, 0:1], i), col_id == place(mt[:, 1:2], i)
            C[0, g, tokens_i, :] = jnp.where(first | second, 1.0, 0.0).astype(BF16)
            weight = jnp.where(first, mt[:, 2:3], 0.0) + jnp.where(second, mt[:, 3:4], 0.0)
            high = weight.astype(BF16)
            C[1, g, tokens_i, :] = high
            C[2, g, tokens_i, :] = (weight - high.astype(F32)).astype(BF16)

    def group(g):
        return slice(16 * g, 16 * g + 16)

    def pick(c, g):
        for a in range(2):
            block = G[c, 4 * g : 4 * g + 4, a].reshape(4 * tok_rows, WIDE)
            picked = dot(D[g], block)
            if a == 1:
                picked = picked * jnp.concatenate([GR[g]] * (WIDE // 128), axis=1)
            S[c, :, a, group(g), :] = picked.astype(BF16).reshape(PLANE, 16, WIDE)
        X[c, 0, :, group(g), :] = S[c, 0, :, group(g), :]

    def send(c, dst, sign, send_sem, recv_sem, g=None):
        rows = slice(0, SOURCE_ROWS) if g is None else group(g)

        def one(j, carry):
            remote(S.at[c, j, :, rows], dst.at[c, j, :, rows], send_sem, recv_sem, in_plane(j, sign)).start()
            return carry

        lax.fori_loop(1, PLANE, one, 0)

    def all_of(c, dst, send_sem, recv_sem, g=None):
        others, rows = pl.ds(1, PLANE - 1), slice(0, SOURCE_ROWS) if g is None else group(g)
        return remote(S.at[c, others, :, rows], dst.at[c, others, :, rows], send_sem, recv_sem, right)

    def all_out(c):
        return all_of(c, X, out_send.at[c], out_recv.at[c])

    def row_tile(c, a, m):
        return X[c, pl.ds(8 * m, 8), a].reshape(8 * SOURCE_ROWS, WIDE)

    def tile_rows(m):
        return pl.ds(pl.multiple_of(m * 256, 256), 256)

    def unit_cols(i):
        units = WB.shape[2]
        return slice(i * units, (i + 1) * units)

    def before_act(c):
        all_out(c).wait_recv()

        def tile(m, carry):
            rows, cots = row_tile(c, 0, m), row_tile(c, 1, m)
            for i, block in enumerate((rows, rows, cots)):
                F[tile_rows(m), unit_cols(i)] += dot_nt(block, WB[i, c])
            return carry

        lax.fori_loop(0, 4, tile, 0)

    def send_out(c, g=None):
        send(c, X, 1, out_send.at[c], out_recv.at[c], g)

    build_pick(0)
    ring_hop(0, 3)
    ring_hop(1, 1)
    pick(0, 0)
    send_out(0, 0)
    build_pick(1)
    ring_hop(0, 4)
    ring_hop(1, 2)
    F[...] = jnp.zeros(F.shape, F32)
    ring_hop(2, 1)
    ring_end(0)
    pick(0, 1)
    send_out(0, 1)
    ring_hop(1, 3)
    ring_hop(1, 4)
    pltpu.make_async_copy(WB, WB, wload_sem).wait()

    def way_out(t, carry):
        @pl.when(t + 2 < n)
        def _():
            ring_hop(t + 2, 1)

        @pl.when(t + 1 < n)
        def _():
            ring_hop(t + 1, 2)

        ring_end(t)
        pick(t, 0)
        pick(t, 1)
        send_out(t)

        @pl.when(t + 1 < n)
        def _():
            ring_hop(t + 1, 3)

        @pl.when(t >= 2)
        def _():
            before_act(t - 2)

        @pl.when(t + 1 < n)
        def _():
            ring_hop(t + 1, 4)

        return carry

    lax.fori_loop(1, n, way_out, 0)
    build_put(0)
    build_put(1)
    before_act(n - 2)
    before_act(n - 1)

    def activate(m, carry):
        pre_gate, pre_up, hidden_grad = (F[tile_rows(m), unit_cols(i)] for i in range(3))
        sigmoid = jax.nn.sigmoid(pre_gate)
        silu = pre_gate * sigmoid
        hidden = silu * pre_up
        gate_grad = hidden_grad * pre_up * (sigmoid * (1.0 + pre_gate * (1.0 - sigmoid)))
        up_grad = hidden_grad * silu
        for i, v in enumerate((gate_grad, up_grad, hidden)):
            H[i, m] = v.astype(BF16)
            T[i, m] = jnp.transpose(v).astype(BF16)
        return carry

    lax.fori_loop(0, 4, activate, 0)

    def answer(c, carry):
        all_out(c).wait_send()

        def tile(m, carry):
            expert_out = dot(H[2, m], WB[2, c])
            row_grad = dot(H[0, m], WB[0, c]) + dot(H[1, m], WB[1, c])
            S[c, pl.ds(8 * m, 8), 0] = expert_out.astype(BF16).reshape(8, SOURCE_ROWS, WIDE)
            S[c, pl.ds(8 * m, 8), 1] = row_grad.astype(BF16).reshape(8, SOURCE_ROWS, WIDE)
            return carry

        lax.fori_loop(0, 4, tile, 0)
        Q[c, 0] = S[c, 0]

        @pl.when(c < n - 1)
        def _():
            send(c, Q, -1, back_send.at[c], back_recv.at[c])

        return carry

    lax.fori_loop(0, n, answer, 0)
    for g in (1, 0):
        send(n - 1, Q, -1, back_send.at[n - 1 + g], back_recv.at[n - 1 + g], g)

    def ring_sent(c, carry):
        for hop in range(1, 5):
            for a in range(2):
                for copy in ring_copies(c, hop, a):
                    copy.wait_send()
        return carry

    lax.fori_loop(0, n, ring_sent, 0)

    def part(c, slot, a):
        g, frames = slot // 4, slice((slot % 4) * tok_rows, (slot % 4 + 1) * tok_rows)
        rows = Q[c, :, a, group(g), :].reshape(half, WIDE)
        if a == 0:
            return dot(C[1, g, frames, :], rows) + dot(C[2, g, frames, :], rows)
        return dot(C[0, g, frames, :], rows)

    def rs_copies(c, hop, a):
        if hop == 1:
            return [remote(G.at[c, 7, a], RS.at[c, a, 3, a], rs_send.at[c, a, 3, a], rs_recv.at[c, a, 3, a], (right, left)[a])]
        at, to = 5 - hop, 4 - hop
        return [
            remote(RS.at[c, way, at, a], RS.at[c, way, to, a], rs_send.at[c, way, to, a], rs_recv.at[c, way, to, a], whom)
            for way, whom in enumerate((right, left))
        ]

    def rs_hop(c, hop):
        for a in range(2):
            copies = rs_copies(c, hop, a)
            if hop == 1:
                G[c, 7, a] = part(c, 7, a).astype(BF16)
                copies[0].start()
                continue
            at = 5 - hop
            for way, slots in enumerate((FROM_RIGHT, FROM_LEFT)):
                total = part(c, slots[at], a)
                if hop > 2:
                    rs_copies(c, hop - 1, a)[way].wait_recv()
                elif a == way:
                    rs_copies(c, 1, a)[0].wait_recv()
                if hop > 2 or a == way:
                    total = total + RS[c, way, at, a].astype(F32)
                RS[c, way, at, a] = total.astype(BF16)
                copies[way].start()

    def stores(c):
        return [
            pltpu.make_async_copy(G.at[c, 0, a], ref.at[:, columns(c)], store_sem.at[c, a])
            for a, ref in enumerate((layer_out, token_grad))
        ]

    def rs_end(c):
        for a, copy in enumerate(stores(c)):
            total = part(c, 0, a)
            for way in range(2):
                rs_copies(c, 4, a)[way].wait_recv()
                total = total + RS[c, way, 0, a].astype(F32)
            G[c, 0, a] = total.astype(BF16)
            copy.start()

    def wstore(c, i):
        ref = (grad_gate, grad_up, grad_down)[i]
        return pltpu.make_async_copy(WB.at[i, c], ref.at[0, :, columns(c)], wstore_sem.at[c, i])

    def weight_grad(c, i):
        a = 1 if i == 2 else 0
        total = dot(T[i, 0], row_tile(c, a, 0))
        for m in range(1, 4):
            total += dot(T[i, m], row_tile(c, a, m))
        WB[i, c] = total.astype(BF16)
        wstore(c, i).start()

    def all_back(c, number, g=None):
        return all_of(c, Q, back_send.at[number], back_recv.at[number], g)

    def way_back(c, carry):
        all_back(c, c).wait_recv()
        rs_hop(c, 1)

        @pl.when(c >= 1)
        def _():
            rs_hop(c - 1, 3)

        @pl.when(c >= 2)
        def _():
            rs_end(c - 2)

        for i in range(3):
            weight_grad(c, i)
        rs_hop(c, 2)

        @pl.when(c >= 1)
        def _():
            rs_hop(c - 1, 4)

        return carry

    lax.fori_loop(0, n - 1, way_back, 0)
    rs_hop(n - 2, 3)
    rs_end(n - 3)
    for i in range(3):
        weight_grad(n - 1, i)
    rs_hop(n - 2, 4)
    all_back(n - 1, n, 1).wait_recv()
    rs_hop(n - 1, 1)
    rs_hop(n - 1, 2)
    rs_end(n - 2)
    all_back(n - 1, n - 1, 0).wait_recv()
    rs_hop(n - 1, 3)
    rs_hop(n - 1, 4)
    rs_end(n - 1)

    def finish(c, carry):
        for copy in stores(c):
            copy.wait()
        for i in range(3):
            wstore(c, i).wait()
        for hop in range(1, 5):
            for a in range(2):
                for copy in rs_copies(c, hop, a):
                    copy.wait_send()

        @pl.when(c < n - 1)
        def _():
            all_back(c, c).wait_send()

        return carry

    lax.fori_loop(0, n, finish, 0)
    for g in range(2):
        all_back(n - 1, n - 1 + g, g).wait_send()
    for copy in metas:
        copy.wait_send()


PIECES = 4


def hand_over(*refs):
    results, outs, held, in_sem, out_sem = refs[:5], refs[5:10], refs[10:15], refs[15], refs[16]
    ins, backs = [], []
    for i in (2, 3, 4, 0, 1):
        rows = results[i].shape[-2] // PIECES
        for p in range(PIECES):
            at = (0,) * (len(results[i].shape) - 2) + (pl.ds(p * rows, rows),)
            ins.append(pltpu.make_async_copy(results[i].at[at], held[i].at[at], in_sem.at[i, p]))
            backs.append(pltpu.make_async_copy(held[i].at[at], outs[i].at[at], out_sem.at[i, p]))
    for copy in ins:
        copy.start()
    for copy, back in zip(ins, backs):
        copy.wait()
        back.start()
    for back in backs:
        back.wait()


def local(tokens, cotangent, expert_ids, gate_values, w_gate, w_up, w_down):
    tok_rows, width = tokens.shape
    hidden = w_gate.shape[1]
    n = width // WIDE
    rows = PLANE * SOURCE_ROWS
    half = PLANE * 16
    sem = pltpu.SemaphoreType.DMA
    vmem, hbm = pl.BlockSpec(memory_space=pltpu.VMEM), pl.BlockSpec(memory_space=pl.ANY)
    results = pl.pallas_call(
        kernel,
        out_shape=[jax.ShapeDtypeStruct(v.shape, BF16) for v in (tokens, cotangent, w_gate, w_up, w_down)],
        in_specs=[vmem] * 2 + [hbm] * 5,
        out_specs=[hbm] * 5,
        scratch_shapes=[
            pltpu.VMEM((n, RING, 2, tok_rows, WIDE), BF16),
            pltpu.VMEM((n, PLANE, 2, SOURCE_ROWS, WIDE), BF16),
            pltpu.VMEM((n, PLANE, 2, SOURCE_ROWS, WIDE), BF16),
            pltpu.VMEM((n, PLANE, 2, SOURCE_ROWS, WIDE), BF16),
            pltpu.VMEM((n, 2, 4, 2, tok_rows, WIDE), BF16),
            pltpu.VMEM((3, n, hidden, WIDE), BF16),
            pltpu.VMEM((rows, 3 * hidden), F32),
            pltpu.VMEM((3, 4, rows // 4, hidden), BF16),
            pltpu.VMEM((3, 4, hidden, rows // 4), BF16),
            pltpu.VMEM((2, half, 4 * tok_rows), BF16),
            pltpu.VMEM((3, 2, 4 * tok_rows, half), BF16),
            pltpu.VMEM((2, half, 128), F32),
            pltpu.VMEM((RING, 8, tok_rows), F32),
            sem((n, 2)), sem, sem((RING,)), sem((RING,)), sem((n, 8, 2)), sem((n, 8, 2)),
            sem((n,)), sem((n,)), sem((n + 1,)), sem((n + 1,)), sem((n, 2, 4, 2)), sem((n, 2, 4, 2)), sem((n, 2)), sem((n, 3)),
        ],
        compiler_params=pltpu.CompilerParams(
            collective_id=0, has_side_effects=True, vmem_limit_bytes=63 * 2**20
        ),
    )(expert_ids.T, gate_values.T, tokens, cotangent, w_gate, w_up, w_down)
    return pl.pallas_call(
        hand_over,
        out_shape=[jax.ShapeDtypeStruct(v.shape, v.dtype) for v in results],
        in_specs=[pl.BlockSpec(memory_space=pltpu.HBM)] * 5,
        out_specs=[pl.BlockSpec(memory_space=pltpu.HBM)] * 5,
        scratch_shapes=[pltpu.VMEM(v.shape, v.dtype) for v in results] + [sem((5, PIECES)), sem((5, PIECES))],
    )(*results)


def solution(mesh):
    rows = P(("zero", "expert"), None)
    weights = P("expert", "zero", None)
    return jax.shard_map(
        local,
        mesh=mesh,
        in_specs=(rows, rows, rows, rows, weights, weights, weights),
        out_specs=(rows, rows, weights, weights, weights),
        check_vma=False,
    )
```

time: 297 us -> 269 us (0.906); the launches traced: 296 us -> 265 us
  Pallas kernels: 285 us -> 264 us
  local copies, waits for them, and re-layouts: 10.4 us -> 0 us
    pallas_call x1, Pallas kernels: 285 us -> 259 us  [local(): pl.pallas_call(kernel, out_shape=[jax.ShapeDtypeStruct(v.shape, BF16) for...]
    unnamed x12 -> x0, local copies, waits for them, and re-layouts: 10.4 us -> none
    pallas_call x0 -> x1, Pallas kernels: none -> 5.16 us  [local(): pl.pallas_call(hand_over, out_shape=[jax.ShapeDtypeStruct(v.shape, v.dtyp...]
where the time goes in v2:
time: 269 us; the launch traced here: 265 us
  Pallas kernels  264 us (98%)
    pallas_call x1, Pallas kernels, local(): pl.pallas_call(kernel, out_shape=[jax.ShapeDtypeStruct(v.shape, BF16) for...  259 us

profile of v2, /device:TPU:56, one launch (start us, length us, event | category | flops | bytes accessed | tf_op | source)
XLA Modules:
  0.0 264.7 jit_solution(15586572282415797861)
XLA Ops:
  0.6 258.7 %shard_map.110 = (bf16[128,2048]{1,0:T(8,128)(2,1)}, bf16[128,2048]{1,0:T(8,128)(2,1)}, bf16[1,384,2048]{2,1,0:T(8,128)(2,1)}, bf16[1,384,2048]{2,1,0:T(8,128)(2,1)}, bf16[1,384,2048]{2,1,0:T(8,128)(2,1)}) custom-call(s32[2,128]{1,0:T(2,128)} %bitcast.2, f32[2,128]{1,0:T(2,128)} %bitcast.3, bf16[128,2048]{1,0:T(8,128)(2,1)} %tok.1, bf16[128,2048]{1,0:T(8,128)(2,1)} %cot.1, ...), custom_call_target="tpu_custom_call" | custom-call | tf_op jit(solution)/shard_map/pallas_call | solution.py:492
  259.4 5.2 %shard_map.111 = (bf16[128,2048]{1,0:T(8,128)(2,1)}, bf16[128,2048]{1,0:T(8,128)(2,1)}, bf16[1,384,2048]{2,1,0:T(8,128)(2,1)}, bf16[1,384,2048]{2,1,0:T(8,128)(2,1)}, bf16[1,384,2048]{2,1,0:T(8,128)(2,1)}) custom-call(bf16[128,2048]{1,0:T(8,128)(2,1)} %get-tuple-element.10.refs_0_, bf16[128,2048]{1,0:T(8,128)(2,1)} %get-tuple-element.11.refs_1_, ...), custom_call_target="tpu_custom_call" | custom-call | tf_op jit(solution)/shard_map/pallas_call | solution.py:518

commit v3 on v2

--- a/solution.py
+++ b/solution.py
@@ -14,6 +14,7 @@
 PLANE = 32
 WIDE = 256
 CAP = 4
+LAG = 3
 SOURCE_ROWS = RING * CAP
 FROM_LEFT = {0: 0, 1: 1, 2: 3, 3: 5, 4: 7}
 FROM_RIGHT = {0: 0, 1: 2, 2: 4, 3: 6, 4: 7}
@@ -67,8 +68,7 @@
             copy.start()
         return carry
 
-    lax.fori_loop(0, n, start_load, 0)
-
+    start_load(0, 0)
     barrier = pltpu.get_barrier_semaphore()
 
     def greet(j, carry):
@@ -83,8 +83,6 @@
         for i, ref in enumerate((wg, wu, wd)):
             pltpu.make_async_copy(ref.at[0, :, columns(c)], WB.at[i, c], wload_sem).start()
         return carry
-
-    lax.fori_loop(0, n, start_weights, 0)
 
     earlier = lax.broadcasted_iota(I32, (tok_rows, tok_rows), 0) < lax.broadcasted_iota(
         I32, (tok_rows, tok_rows), 1
@@ -151,6 +149,7 @@
             metas.append(remote(M.at[0], M.at[slot], meta_send.at[slot], meta_recv.at[slot], along_z(step)))
     for copy in metas:
         copy.start()
+    lax.fori_loop(1, n, start_load, 0)
     ring_hop(0, 2)
     for copy in metas:
         copy.wait_recv()
@@ -201,7 +200,8 @@
     def send(c, dst, sign, send_sem, recv_sem, g=None):
         rows = slice(0, SOURCE_ROWS) if g is None else group(g)
 
-        def one(j, carry):
+        def one(k, carry):
+            j = (k * 11) % PLANE
             remote(S.at[c, j, :, rows], dst.at[c, j, :, rows], send_sem, recv_sem, in_plane(j, sign)).start()
             return carry
 
@@ -243,43 +243,38 @@
     ring_hop(1, 1)
     pick(0, 0)
     send_out(0, 0)
+    lax.fori_loop(0, n, start_weights, 0)
     build_pick(1)
     ring_hop(0, 4)
     ring_hop(1, 2)
+    ring_hop(2, 1)
     F[...] = jnp.zeros(F.shape, F32)
-    ring_hop(2, 1)
     ring_end(0)
     pick(0, 1)
     send_out(0, 1)
     ring_hop(1, 3)
+    ring_hop(2, 2)
+    ring_hop(3, 1)
     ring_hop(1, 4)
+    ring_hop(2, 3)
+    ring_hop(3, 2)
+    ring_hop(4, 1)
     pltpu.make_async_copy(WB, WB, wload_sem).wait()
 
     def way_out(t, carry):
-        @pl.when(t + 2 < n)
-        def _():
-            ring_hop(t + 2, 1)
-
-        @pl.when(t + 1 < n)
-        def _():
-            ring_hop(t + 1, 2)
-
         ring_end(t)
         pick(t, 0)
         pick(t, 1)
         send_out(t)
-
-        @pl.when(t + 1 < n)
-        def _():
-            ring_hop(t + 1, 3)
+        for ahead in range(1, 5):
+
+            @pl.when(t + ahead < n)
+            def _(ahead=ahead):
+                ring_hop(t + ahead, 5 - ahead)
 
         @pl.when(t >= 2)
         def _():
             before_act(t - 2)
-
-        @pl.when(t + 1 < n)
-        def _():
-            ring_hop(t + 1, 4)
 
         return carry
 
@@ -351,7 +346,7 @@
             for way, whom in enumerate((right, left))
         ]
 
-    def rs_hop(c, hop):
+    def rs_hop(c, hop, ways=(0, 1)):
         for a in range(2):
             copies = rs_copies(c, hop, a)
             if hop == 1:
@@ -359,8 +354,8 @@
                 copies[0].start()
                 continue
             at = 5 - hop
-            for way, slots in enumerate((FROM_RIGHT, FROM_LEFT)):
-                total = part(c, slots[at], a)
+            for way in ways:
+                total = part(c, (FROM_RIGHT, FROM_LEFT)[way][at], a)
                 if hop > 2:
                     rs_copies(c, hop - 1, a)[way].wait_recv()
                 elif a == way:
@@ -399,43 +394,6 @@
 
     def all_back(c, number, g=None):
         return all_of(c, Q, back_send.at[number], back_recv.at[number], g)
-
-    def way_back(c, carry):
-        all_back(c, c).wait_recv()
-        rs_hop(c, 1)
-
-        @pl.when(c >= 1)
-        def _():
-            rs_hop(c - 1, 3)
-
-        @pl.when(c >= 2)
-        def _():
-            rs_end(c - 2)
-
-        for i in range(3):
-            weight_grad(c, i)
-        rs_hop(c, 2)
-
-        @pl.when(c >= 1)
-        def _():
-            rs_hop(c - 1, 4)
-
-        return carry
-
-    lax.fori_loop(0, n - 1, way_back, 0)
-    rs_hop(n - 2, 3)
-    rs_end(n - 3)
-    for i in range(3):
-        weight_grad(n - 1, i)
-    rs_hop(n - 2, 4)
-    all_back(n - 1, n, 1).wait_recv()
-    rs_hop(n - 1, 1)
-    rs_hop(n - 1, 2)
-    rs_end(n - 2)
-    all_back(n - 1, n - 1, 0).wait_recv()
-    rs_hop(n - 1, 3)
-    rs_hop(n - 1, 4)
-    rs_end(n - 1)
 
     def finish(c, carry):
         for copy in stores(c):
@@ -453,7 +411,49 @@
 
         return carry
 
-    lax.fori_loop(0, n, finish, 0)
+    def way_back(c, carry):
+        all_back(c, c).wait_recv()
+        rs_hop(c, 1)
+
+        @pl.when(c >= 1)
+        def _():
+            rs_hop(c - 1, 3)
+
+        @pl.when(c >= 2)
+        def _():
+            rs_end(c - 2)
+
+        for i in range(3):
+            weight_grad(c, i)
+        rs_hop(c, 2)
+
+        @pl.when(c >= 1)
+        def _():
+            rs_hop(c - 1, 4)
+
+        @pl.when(c >= LAG)
+        def _():
+            finish(c - LAG, 0)
+
+        return carry
+
+    lax.fori_loop(0, n - 1, way_back, 0)
+    all_back(n - 1, n, 1).wait_recv()
+    rs_hop(n - 1, 1)
+    rs_hop(n - 2, 3)
+    rs_end(n - 3)
+    rs_hop(n - 1, 2)
+    rs_hop(n - 2, 4)
+    rs_hop(n - 1, 3, (0,))
+    all_back(n - 1, n - 1, 0).wait_recv()
+    rs_hop(n - 1, 3, (1,))
+    for i in range(3):
+        weight_grad(n - 1, i)
+    rs_end(n - 2)
+    rs_hop(n - 1, 4)
+    lax.fori_loop(n - LAG - 1, n - 1, finish, 0)
+    rs_end(n - 1)
+    finish(n - 1, 0)
     for g in range(2):
         all_back(n - 1, n - 1 + g, g).wait_send()
     for copy in metas:

time: 269 us -> 258 us (0.959)
  Pallas kernels: 264 us -> 253 us
    pallas_call x1, Pallas kernels: 259 us -> 248 us  [local(): pl.pallas_call(kernel, out_shape=[jax.ShapeDtypeStruct(v.shape, BF16) for...]
where the time goes in v3:
time: 258 us; the launch traced here: 254 us
  Pallas kernels  253 us (98%)
    pallas_call x1, Pallas kernels, local(): pl.pallas_call(kernel, out_shape=[jax.ShapeDtypeStruct(v.shape, BF16) for...  248 us
    pallas_call x1, Pallas kernels, local(): pl.pallas_call(hand_over, out_shape=[jax.ShapeDtypeStruct(v.shape, v.dtyp...  5.16 us

profile of v3, /device:TPU:56, one launch (start us, length us, event | category | flops | bytes accessed | tf_op | source)
XLA Modules:
  0.0 254.0 jit_solution(2281633208655836445)
XLA Ops:
  0.6 248.1 %shard_map.110 = (bf16[128,2048]{1,0:T(8,128)(2,1)}, bf16[128,2048]{1,0:T(8,128)(2,1)}, bf16[1,384,2048]{2,1,0:T(8,128)(2,1)}, bf16[1,384,2048]{2,1,0:T(8,128)(2,1)}, bf16[1,384,2048]{2,1,0:T(8,128)(2,1)}) custom-call(s32[2,128]{1,0:T(2,128)} %bitcast.2, f32[2,128]{1,0:T(2,128)} %bitcast.3, bf16[128,2048]{1,0:T(8,128)(2,1)} %tok.1, bf16[128,2048]{1,0:T(8,128)(2,1)} %cot.1, ...), custom_call_target="tpu_custom_call" | custom-call | tf_op jit(solution)/shard_map/pallas_call | solution.py:492
  248.7 5.2 %shard_map.111 = (bf16[128,2048]{1,0:T(8,128)(2,1)}, bf16[128,2048]{1,0:T(8,128)(2,1)}, bf16[1,384,2048]{2,1,0:T(8,128)(2,1)}, bf16[1,384,2048]{2,1,0:T(8,128)(2,1)}, bf16[1,384,2048]{2,1,0:T(8,128)(2,1)}) custom-call(bf16[128,2048]{1,0:T(8,128)(2,1)} %get-tuple-element.10.refs_0_, bf16[128,2048]{1,0:T(8,128)(2,1)} %get-tuple-element.11.refs_1_, ...), custom_call_target="tpu_custom_call" | custom-call | tf_op jit(solution)/shard_map/pallas_call | solution.py:518

commit v4 on v3

--- a/solution.py
+++ b/solution.py
@@ -311,7 +311,7 @@
         lax.fori_loop(0, 4, tile, 0)
         Q[c, 0] = S[c, 0]
 
-        @pl.when(c < n - 1)
+        @pl.when(c < n - 2)
         def _():
             send(c, Q, -1, back_send.at[c], back_recv.at[c])
 
@@ -319,7 +319,8 @@
 
     lax.fori_loop(0, n, answer, 0)
     for g in (1, 0):
-        send(n - 1, Q, -1, back_send.at[n - 1 + g], back_recv.at[n - 1 + g], g)
+        for c in (n - 2, n - 1):
+            send(c, Q, -1, back_send.at[c + 2 * g], back_recv.at[c + 2 * g], g)
 
     def ring_sent(c, carry):
         for hop in range(1, 5):
@@ -405,7 +406,7 @@
                 for copy in rs_copies(c, hop, a):
                     copy.wait_send()
 
-        @pl.when(c < n - 1)
+        @pl.when(c < n - 2)
         def _():
             all_back(c, c).wait_send()
 
@@ -437,25 +438,39 @@
 
         return carry
 
-    lax.fori_loop(0, n - 1, way_back, 0)
-    all_back(n - 1, n, 1).wait_recv()
+    def half_back(c, g):
+        return all_back(c, c + 2 * g, g)
+
+    lax.fori_loop(0, n - 2, way_back, 0)
+    half_back(n - 2, 1).wait_recv()
+    rs_hop(n - 2, 1)
+    rs_hop(n - 3, 3)
+    rs_end(n - 4)
+    for i in range(3):
+        weight_grad(n - 2, i)
+    rs_hop(n - 2, 2)
+    rs_hop(n - 3, 4)
+    half_back(n - 1, 1).wait_recv()
     rs_hop(n - 1, 1)
-    rs_hop(n - 2, 3)
+    rs_hop(n - 2, 3, (0,))
+    half_back(n - 2, 0).wait_recv()
+    rs_hop(n - 2, 3, (1,))
     rs_end(n - 3)
     rs_hop(n - 1, 2)
     rs_hop(n - 2, 4)
     rs_hop(n - 1, 3, (0,))
-    all_back(n - 1, n - 1, 0).wait_recv()
+    half_back(n - 1, 0).wait_recv()
     rs_hop(n - 1, 3, (1,))
     for i in range(3):
         weight_grad(n - 1, i)
     rs_end(n - 2)
     rs_hop(n - 1, 4)
-    lax.fori_loop(n - LAG - 1, n - 1, finish, 0)
+    lax.fori_loop(n - LAG - 2, n - 1, finish, 0)
     rs_end(n - 1)
     finish(n - 1, 0)
-    for g in range(2):
-        all_back(n - 1, n - 1 + g, g).wait_send()
+    for c in (n - 2, n - 1):
+        for g in range(2):
+            half_back(c, g).wait_send()
     for copy in metas:
         copy.wait_send()
 
@@ -509,7 +524,7 @@
             pltpu.VMEM((2, half, 128), F32),
             pltpu.VMEM((RING, 8, tok_rows), F32),
             sem((n, 2)), sem, sem((RING,)), sem((RING,)), sem((n, 8, 2)), sem((n, 8, 2)),
-            sem((n,)), sem((n,)), sem((n + 1,)), sem((n + 1,)), sem((n, 2, 4, 2)), sem((n, 2, 4, 2)), sem((n, 2)), sem((n, 3)),
+            sem((n,)), sem((n,)), sem((n + 2,)), sem((n + 2,)), sem((n, 2, 4, 2)), sem((n, 2, 4, 2)), sem((n, 2)), sem((n, 3)),
         ],
         compiler_params=pltpu.CompilerParams(
             collective_id=0, has_side_effects=True, vmem_limit_bytes=63 * 2**20

time: 258 us -> 257 us (level)
  no operation moved by 1% of the time
where the time goes in v4:
time: 257 us; the launch traced here: 253 us
  Pallas kernels  252 us (98%)
    pallas_call x1, Pallas kernels, local(): pl.pallas_call(kernel, out_shape=[jax.ShapeDtypeStruct(v.shape, BF16) for...  247 us
    pallas_call x1, Pallas kernels, local(): pl.pallas_call(hand_over, out_shape=[jax.ShapeDtypeStruct(v.shape, v.dtyp...  5.16 us

profile of v4, /device:TPU:56, one launch (start us, length us, event | category | flops | bytes accessed | tf_op | source)
XLA Modules:
  0.0 252.7 jit_solution(9481999400358289804)
XLA Ops:
  0.6 246.7 %shard_map.110 = (bf16[128,2048]{1,0:T(8,128)(2,1)}, bf16[128,2048]{1,0:T(8,128)(2,1)}, bf16[1,384,2048]{2,1,0:T(8,128)(2,1)}, bf16[1,384,2048]{2,1,0:T(8,128)(2,1)}, bf16[1,384,2048]{2,1,0:T(8,128)(2,1)}) custom-call(s32[2,128]{1,0:T(2,128)} %bitcast.2, f32[2,128]{1,0:T(2,128)} %bitcast.3, bf16[128,2048]{1,0:T(8,128)(2,1)} %tok.1, bf16[128,2048]{1,0:T(8,128)(2,1)} %cot.1, ...), custom_call_target="tpu_custom_call" | custom-call | tf_op jit(solution)/shard_map/pallas_call | solution.py:507
  247.4 5.2 %shard_map.111 = (bf16[128,2048]{1,0:T(8,128)(2,1)}, bf16[128,2048]{1,0:T(8,128)(2,1)}, bf16[1,384,2048]{2,1,0:T(8,128)(2,1)}, bf16[1,384,2048]{2,1,0:T(8,128)(2,1)}, bf16[1,384,2048]{2,1,0:T(8,128)(2,1)}) custom-call(bf16[128,2048]{1,0:T(8,128)(2,1)} %get-tuple-element.10.refs_0_, bf16[128,2048]{1,0:T(8,128)(2,1)} %get-tuple-element.11.refs_1_, ...), custom_call_target="tpu_custom_call" | custom-call | tf_op jit(solution)/shard_map/pallas_call | solution.py:533
